TPU v7x, 32 devices: a whole 2x2x4 slice. The times are simulated.
32 devices in a mesh: sub: 16 (over z, y, x), panel: 2 (over core).
Axes of the slice: x: 2, y: 2, z: 4, core: 2. Of those that a mesh axis runs over, the one named last changes fastest.
Arguments:
- stiffness_tiles: bfloat16 [256, 8, 128, 128], P('sub'), may hold values from -0.1875 to 0.1875
- tile_columns: int32 [256, 8], P('sub'), may hold values from 0 to 19
- tile_counts: int32 [16, 16], P('sub'), may hold values from 1 to 8, 96 in all within a row
- phi_modes: bfloat16 [32768, 2048], P('sub', 'panel'), may hold values from -1.5 to 1.5
- halo_to_right: int32 [32], P('sub'), may hold values from 0 to 15
- halo_to_left: int32 [32], P('sub'), may hold values from 0 to 15
- liner_rows: int32 [8192], P('sub'), may hold values from 0 to 2047
- liner_owner: int32 [8192, 1], P('sub'), may hold values from 0 to 15; in each aligned block of 512 rows (0 to 511, 512 to 1023, ...) at most 32 rows name the same one
- liner_slot: int32 [8192], P('sub'), may hold values from 0 to 31
Outputs:
- reduced: float32 [2048, 2048], P('sub', 'panel')
- interface_load: float32 [512, 2048], P('sub', 'panel')
Inputs may be any that keep to these rules, and one draw needn't show every extreme that they name: `tile_counts`: counts a slab's used slots; the counts of one slab sum to 96. `tile_columns`: indices into the slab's extended tiles. `liner_owner`: among the listed rows of one slab at most 32 name one owner, and in every draw some owner is named by exactly 32 rows of some slab.
All inputs are finite; a program needn't handle non-finite values.
Results may differ from a plain program's by a relative error of at most 0.0029.
Values may be sent and summed in bfloat16 or wider, within the bound.
A program may use at most 128 MiB of HBM per device.

v0:
```python
import jax
import jax.numpy as jnp
from jax import lax
from jax.sharding import PartitionSpec as P

CAP = 32
IF_DEV = 32


def shifted(value, axis, steps):
    count = lax.axis_size(axis)
    initial, last = (max(0, -steps), min(count, count - steps))
    return lax.ppermute(value, axis, [(source, source + steps) for source in range(initial, last)])


def body(
    stiffness_tiles,
    tile_columns,
    tile_counts,
    phi_modes,
    halo_to_right,
    halo_to_left,
    liner_rows,
    liner_owner,
    liner_slot,
):
    block_rows, slot_count, tile_size = (
        stiffness_tiles.shape[0],
        stiffness_tiles.shape[1],
        stiffness_tiles.shape[2],
    )
    slab_rows, panel_width = phi_modes.shape
    phi_tiles = phi_modes.reshape(block_rows, tile_size, panel_width)
    left_halo = shifted(phi_tiles[halo_to_right], "sub", 1)
    right_halo = shifted(phi_tiles[halo_to_left], "sub", -1)
    extended = jnp.concatenate([left_halo, phi_tiles, right_halo], axis=0)
    usable = jnp.arange(slot_count, dtype=jnp.int32)[None, :] < tile_counts[0][:, None]
    chosen = jnp.where(
        usable[:, :, None, None], extended[tile_columns], jnp.zeros((), jnp.bfloat16)
    )
    kphi = jnp.einsum("bjrc,bjcw->brw", stiffness_tiles, chosen, preferred_element_type=jnp.float32)
    kphi = kphi.astype(jnp.bfloat16).reshape(slab_rows, panel_width)
    partial_value = lax.dot_general(
        lax.all_gather(phi_modes, "panel", axis=1, tiled=True),
        kphi,
        (((0,), (0,)), ((), ())),
        preferred_element_type=jnp.float32,
    )
    reduced = lax.psum_scatter(partial_value, "sub", scatter_dimension=0, tiled=True)
    owners = liner_owner[:, 0]
    picked = kphi[liner_rows]
    sub_count = lax.axis_size("sub")
    member = (owners[:, None] == jnp.arange(sub_count, dtype=jnp.int32)[None, :]).astype(jnp.int32)
    before = jnp.cumsum(member, axis=0) - member
    position = jnp.sum(before * member, axis=1)
    destination = owners * CAP + position
    placement_table = jnp.arange(sub_count * CAP, dtype=jnp.int32)[:, None] == destination[None, :]
    outbox = jnp.dot(
        placement_table.astype(jnp.bfloat16), picked, preferred_element_type=jnp.float32
    )
    outbox = outbox.astype(jnp.bfloat16).reshape(sub_count, CAP, panel_width)
    slot_box = jnp.sum(jnp.where(placement_table, liner_slot[None, :] + 1, 0), axis=1) - 1
    slot_box = slot_box.reshape(sub_count, CAP)
    inbox, slot_in = (
        lax.all_to_all(outbox, "sub", split_axis=0, concat_axis=0, tiled=True),
        lax.all_to_all(slot_box, "sub", split_axis=0, concat_axis=0, tiled=True),
    )
    arrived = inbox.reshape(sub_count * CAP, panel_width)
    selector = (
        jnp.arange(IF_DEV, dtype=jnp.int32)[:, None] == slot_in.reshape(1, sub_count * CAP)
    ).astype(jnp.bfloat16)
    interface_load = jnp.dot(selector, arrived, preferred_element_type=jnp.float32)
    return (reduced, interface_load)


def solution(mesh):
    return jax.shard_map(
        body,
        mesh=mesh,
        in_specs=(
            P("sub", None, None, None),
            P("sub", None),
            P("sub", None),
            P("sub", "panel"),
            P("sub"),
            P("sub"),
            P("sub"),
            P("sub", None),
            P("sub"),
        ),
        out_specs=(P("sub", "panel"), P("sub", "panel")),
        check_vma=False,
    )
```

profile of v0, /device:TPU:10, one launch (start us, length us, event | category | flops | bytes accessed | tf_op | source)
XLA Modules:
  0.0 291.1 jit_solution(10314754397405650685)
XLA Ops:
  7.2 0.7 all-gather.2.cloned.1.call-update
  8.0 0.7 compare_select_fusion.3
  8.6 2.8 gather_fusion
  11.4 3.4 %collective-permute-start = (bf16[2,128,1024]{2,1,0:T(8,128)(2,1)S(1)}, bf16[2,128,1024]{2,1,0:T(8,128)(2,1)S(1)}, u32[]{:S(2)}, u32[]{:S(2)}) collective-permute-start(bf16[2,128,1024]{2,1,0:T(8,128)(2,1)S(1)} %gather_fusion), channel_id=1, source_target_pairs={{0,2},{2,4},{4,6},{6,8},{8,10},{10,12},{12,14},{14,16},{16,18},{18... | collective-permute-start | bytes 1572872 | tf_op jit(solution)/shard_map/ppermute | solution.py:13
  14.9 2.9 gather_fusion.1
  17.7 2.4 collective-permute-start.1
  20.2 0.1 copy.16
  20.3 0.1 reshape.108
  20.4 0.1 iota_compare_fusion.6
  20.5 17.7 %collective-permute-done = bf16[2,128,1024]{2,1,0:T(8,128)(2,1)S(1)} collective-permute-done((bf16[2,128,1024]{2,1,0:T(8,128)(2,1)S(1)}, bf16[2,128,1024]{2,1,0:T(8,128)(2,1)S(1)}, u32[]{:S(2)}, u32[]{:S(2)}) %collective-permute-start) | collective-permute-done | bytes 524320 | tf_op jit(solution)/shard_map/ppermute | solution.py:13
  38.2 1.0 collective-permute-done.1
  39.2 5.2 %pad_maximum_fusion = bf16[20,128,1024]{2,1,0:T(8,128)(2,1)} fusion(bf16[2,128,1024]{2,1,0:T(8,128)(2,1)S(1)} %collective-permute-done.1, bf16[16,128,1024]{2,1,0:T(8,128)(2,1)} %bitcast.42, bf16[2,128,1024]{2,1,0:T(8,128)(2,1)S(1)} %collective-permute-done), kind=kLoop, calls=%fused_computation.9 | loop fusion | flops 5242880 | bytes 10485760 | tf_op jit(solution)/shard_map/concatenate | solution.py:36
  44.4 15.3 %gather_fusion.2 = bf16[128,128,1024]{2,1,0:T(8,128)(2,1)} fusion(bf16[20,128,1024]{2,1,0:T(8,128)(2,1)} %pad_maximum_fusion, s32[1024]{0:T(1024)S(1)} %pad_clamp_fusion.1), kind=kCustom, calls=%fused_computation.2 | custom fusion | bytes 67109376 | tf_op jit(solution)/shard_map/gather | solution.py:39
  59.6 15.9 %bitcast_convert_fusion = bf16[16,1024,128]{1,2,0:T(8,128)(2,1)} fusion(bf16[16,8,128,128]{3,2,1,0:T(8,128)(2,1)} %param.9, bf16[16,8,128,1024]{3,2,1,0:T(8,128)(2,1)} %bitcast.39, pred[16,8]{1,0:T(8,128)(4,1)S(1)} %iota_compare_fusion.6), kind=kOutput, calls=%fused_computation.8 | convolution fusion | flops 4313841664 | bytes 41943168 | tf_op jit(solution)/shard_map/bjrc,bjcw->brw/dot_general | solution.py:41
  75.5 14.6 %convolution_bitcast_fusion = f32[2048,1024]{0,1:T(8,128)} fusion(bf16[2048,1024]{1,0:T(8,128)(2,1)} %bitcast.43, bf16[2048,2048]{1,0:T(8,128)(2,1)} %all-gather.2.cloned.1.call-done), kind=kOutput, calls=%fused_computation.10 | convolution fusion | flops 8589934592 | bytes 20971520 | tf_op jit(solution)/shard_map/dot_general | solution.py:43
  90.1 0.6 copy-done
  90.8 1.1 reduce-window.6
  91.9 0.2 slice_reduce_fusion
  92.2 0.1 fusion.10
  92.3 0.2 select_reduce_fusion
  92.5 0.7 sub.11
  93.2 6.2 %all-to-all-start = ((s32[16,1,32]{2,1,0:T(1,128)}), s32[16,1,32]{2,1,0:T(1,128)S(1)}, u32[]{:S(2)}, u32[]{:S(2)}) async-start(s32[16,1,32]{2,1,0:T(1,128)} %sub.11), calls=%async_computation.1 | async-start | bytes 16384 | tf_op jit(solution)/shard_map/all_to_all | solution.py:66
  99.4 5.5 %gather_fusion.3 = bf16[512,1024]{1,0:T(8,128)(2,1)S(1)} fusion(bf16[2048,1024]{1,0:T(8,128)(2,1)} %bitcast.44, s32[1024]{0:T(1024)S(1)} %pad_clamp_fusion), kind=kCustom, calls=%fused_computation.3 | custom fusion | bytes 2099200 | tf_op jit(solution)/shard_map/gather | solution.py:51
  104.9 1.8 convolution_convert_fusion
  106.7 7.0 %all-to-all-start.1 = ((bf16[16,32,1024]{2,1,0:T(8,128)(2,1)}), bf16[16,32,1024]{2,1,0:T(8,128)(2,1)S(1)}, u32[]{:S(2)}, u32[]{:S(2)}) async-start(bf16[16,32,1024]{2,1,0:T(8,128)(2,1)} %bitcast.12), calls=%async_computation.2 | async-start | bytes 2097152 | tf_op jit(solution)/shard_map/all_to_all | solution.py:65
  113.7 0.5 broadcast.84
  114.2 0.7 reduce.5
  114.9 0.1 eq.62
  114.9 30.4 %all-to-all-done.1 = bf16[16,32,1024]{2,1,0:T(8,128)(2,1)S(1)} async-done(((bf16[16,32,1024]{2,1,0:T(8,128)(2,1)}), bf16[16,32,1024]{2,1,0:T(8,128)(2,1)S(1)}, u32[]{:S(2)}, u32[]{:S(2)}) %all-to-all-start.1) | async-done | bytes 1048608 | tf_op jit(solution)/shard_map/all_to_all | solution.py:65
  145.3 0.9 fusion.7
  146.3 136.0 %reduce-scatter.2.cloned.1.call-done = f32[128,1024]{0,1:T(8,128)} async-done(((f32[2048,1024]{0,1:T(8,128)}), f32[128,1024]{0,1:T(8,128)}) %reduce-scatter.2.cloned.1.call-update) | async-done | bytes 524304 | tf_op jit(solution)/shard_map/reduce_scatter | solution.py:49
  282.2 2.0 copy.18
  (28 shorter events, 0.2 us)
Async XLA Ops:
  7.2 7.7 %copy-start.5 = (s32[2]{0:T(128)S(1)}, s32[2]{0:T(128)}, u32[]{:S(2)}) copy-start(s32[2]{0:T(128)} %param.14) | copy-start | bytes 28
  7.2 13.0 %copy-start.1 = (s32[16,8]{0,1:T(8,128)S(1)}, s32[16,8]{0,1:T(8,128)}, u32[]{:S(2)}) copy-start(s32[16,8]{0,1:T(8,128)} %param.10) | copy-start | bytes 1540
  7.2 13.2 %copy-start.4 = (s32[1,16]{1,0:T(1,128)S(1)}, s32[1,16]{1,0:T(1,128)}, u32[]{:S(2)}) copy-start(s32[1,16]{1,0:T(1,128)} %param.11) | copy-start | bytes 196
  7.2 68.3 %all-gather.2.cloned.1.call-start = ((), (), s32[]{:S(2)}) async-start(), calls=%async_computation.3 | async-start | bytes 12582912 | tf_op jit(solution)/shard_map/all_gather | solution.py:44
  7.9 274.3 %reduce-scatter.2.cloned.1.call-start = ((), (), s32[]{:S(2)}) async-start(), calls=%async_computation.4 | async-start | bytes 8912896 | tf_op jit(solution)/shard_map/reduce_scatter | solution.py:49
  11.4 26.8 %collective-permute-start = (bf16[2,128,1024]{2,1,0:T(8,128)(2,1)S(1)}, bf16[2,128,1024]{2,1,0:T(8,128)(2,1)S(1)}, u32[]{:S(2)}, u32[]{:S(2)}) collective-permute-start(bf16[2,128,1024]{2,1,0:T(8,128)(2,1)S(1)} %gather_fusion), channel_id=1, source_target_pairs={{0,2},{2,4},{4,6},{6,8},{8,10},{10,12},{12,14},{14,16},{16,18},{18... | collective-permute-start | bytes 1572872 | tf_op jit(solution)/shard_map/ppermute | solution.py:13
  17.7 21.4 %collective-permute-start.1 = (bf16[2,128,1024]{2,1,0:T(8,128)(2,1)S(1)}, bf16[2,128,1024]{2,1,0:T(8,128)(2,1)S(1)}, u32[]{:S(2)}, u32[]{:S(2)}) collective-permute-start(bf16[2,128,1024]{2,1,0:T(8,128)(2,1)S(1)} %gather_fusion.1), channel_id=1, source_target_pairs={{2,0},{4,2},{6,4},{8,6},{10,8},{12,10},{14,12},{16,14},{18,16},{20... | collective-permute-start | bytes 1572872 | tf_op jit(solution)/shard_map/ppermute | solution.py:13
  90.1 0.7 copy-start
  90.1 2.2 copy-start.2
  90.1 9.3 %copy-start.3 = (s32[512]{0:T(512)S(1)}, s32[512]{0:T(512)}, u32[]{:S(2)}) copy-start(s32[512]{0:T(512)} %param.15) | copy-start | bytes 6148
  93.2 13.5 %all-to-all-start = ((s32[16,1,32]{2,1,0:T(1,128)}), s32[16,1,32]{2,1,0:T(1,128)S(1)}, u32[]{:S(2)}, u32[]{:S(2)}) async-start(s32[16,1,32]{2,1,0:T(1,128)} %sub.11), calls=%async_computation.1 | async-start | bytes 16384 | tf_op jit(solution)/shard_map/all_to_all | solution.py:66
  106.7 38.6 %all-to-all-start.1 = ((bf16[16,32,1024]{2,1,0:T(8,128)(2,1)}), bf16[16,32,1024]{2,1,0:T(8,128)(2,1)S(1)}, u32[]{:S(2)}, u32[]{:S(2)}) async-start(bf16[16,32,1024]{2,1,0:T(8,128)(2,1)} %bitcast.12), calls=%async_computation.2 | async-start | bytes 2097152 | tf_op jit(solution)/shard_map/all_to_all | solution.py:65
Sparse Core Ops, SparseCore 0:
  9.6 21.2 all-gather.1
  90.2 191.9 reduce-scatter.1
where the time goes:
time: 292 us; the launch traced here: 291 us
  waiting for transfers between devices  186 us (64%)
  matrix products  33.2 us (11%)
  local copies, waits for them, and re-layouts  30.7 us (11%)
  starting transfers between devices  19.1 us (7%)
  between operations  14.2 us (5%)
  other arithmetic  8.1 us (3%)
    reduce_scatter x1, waiting for transfers between devices, body(): lax.psum_scatter(partial_value, 'sub', scatter_dimension=0, tiled=True)  136 us
    all_to_all x1, waiting for transfers between devices, body(): lax.all_to_all(outbox, 'sub', split_axis=0, concat_axis=0, tiled=True)  30.4 us
    ppermute x2, waiting for transfers between devices, shifted(): lax.ppermute(value, axis, [(source, source + steps) for source in range(i...  18.7 us
    dot_general x1, matrix products, body(): jnp.einsum('bjrc,bjcw->brw', stiffness_tiles, chosen, preferred_element_t...  15.9 us
    gather x1, local copies, waits for them, and re-layouts, body(): extended[tile_columns]  15.3 us
    dot_general x1, matrix products, body(): lax.dot_general(lax.all_gather(phi_modes, 'panel', axis=1, tiled=True), k...  14.6 us
    all_to_all x1, starting transfers between devices, body(): lax.all_to_all(outbox, 'sub', split_axis=0, concat_axis=0, tiled=True)  6.98 us
    all_to_all x1, starting transfers between devices, body(): lax.all_to_all(slot_box, 'sub', split_axis=0, concat_axis=0, tiled=True)  6.23 us
  transfers between devices with their start and end apart: 6, of which 4 were waited for; matrix products, arithmetic and copies ran while one was open for 19% of the time, Pallas kernels for 0%

commit v1 on v0

v1 whole, which is shorter than its diff:
```python
import functools

import jax
import jax.numpy as jnp
from jax import lax
from jax.experimental import pallas as pl
from jax.experimental.pallas import tpu as pltpu
from jax.sharding import PartitionSpec as P

IF_DEV = 32
LOW = 4
MESH = pl.DeviceIdType.MESH


def kernel(
    n_sub,
    n_panel,
    cols_ref,
    counts_ref,
    to_right_ref,
    to_left_ref,
    rows_ref,
    target_ref,
    tiles_hbm,
    phi_hbm,
    red_ref,
    load_ref,
    ext,
    tiles,
    onehot,
    lhs,
    kphi,
    part,
    halo_out,
    s1_out,
    s1_in,
    s2_out,
    s2_in,
    z_out,
    z_in,
    local_sem,
    halo_send,
    halo_recv,
    pan_send,
    pan_recv,
    s1_send,
    s1_recv,
    s2_send,
    s2_recv,
    z_send,
    z_recv,
):
    block_rows, slots, tile, _ = tiles.shape
    halo = halo_out.shape[1]
    rows = block_rows * tile
    width = kphi.shape[1]
    high = n_sub // LOW
    mode_rows = red_ref.shape[0]
    out_rows = mode_rows + IF_DEV
    per_panel = high // n_panel
    sub = lax.axis_index("sub")
    panel = lax.axis_index("panel")
    low, my_high = lax.rem(sub, LOW), sub // LOW
    bit0, bit1 = lax.rem(low, 2), low // 2
    swap = lax.rem(panel, 2)
    first_bit = (1 - swap) * bit0 + swap * bit1
    second_bit = (1 - swap) * bit1 + swap * bit0
    first_weight, second_weight = 1 + swap, 2 - swap
    first_peer = sub + (1 - 2 * first_bit) * first_weight
    second_peer = sub + (1 - 2 * second_bit) * second_weight

    phi_copy = pltpu.make_async_copy(
        phi_hbm, ext.at[pl.ds(halo, block_rows)], local_sem.at[0]
    )
    tile_copy = pltpu.make_async_copy(tiles_hbm, tiles, local_sem.at[1])
    phi_copy.start()
    tile_copy.start()
    phi_copy.wait()
    for i in range(halo):
        halo_out[0, i] = ext[halo + to_right_ref[i]]
        halo_out[1, i] = ext[halo + to_left_ref[i]]
    zero_tiles = jnp.zeros((halo, tile, width), ext.dtype)

    @pl.when(sub == 0)
    def _():
        ext[pl.ds(0, halo)] = zero_tiles

    @pl.when(sub == n_sub - 1)
    def _():
        ext[pl.ds(halo + block_rows, halo)] = zero_tiles

    barrier = pltpu.get_barrier_semaphore()

    def greet(place):
        pl.semaphore_signal(barrier, inc=1, device_id=place, device_id_type=MESH)

    greet({"sub": first_peer, "panel": panel})
    greet({"sub": second_peer, "panel": panel})

    @pl.when(sub > 0)
    def _():
        greet({"sub": sub - 1, "panel": panel})

    @pl.when(sub < n_sub - 1)
    def _():
        greet({"sub": sub + 1, "panel": panel})

    for step in range(1, n_panel):
        greet({"sub": sub, "panel": lax.rem(panel + step, n_panel)})
    for step in range(1, high):
        greet({"sub": lax.rem(my_high + step, high) * LOW + low, "panel": panel})
    ends = jnp.where(sub > 0, 1, 0) + jnp.where(sub < n_sub - 1, 1, 0)
    pl.semaphore_wait(barrier, 2 + (n_panel - 1) + (high - 1) + ends)

    def halo_copy(side):
        return pltpu.make_async_remote_copy(
            src_ref=halo_out.at[side],
            dst_ref=ext.at[pl.ds(side * (halo + block_rows), halo)],
            send_sem=halo_send.at[side],
            recv_sem=halo_recv.at[side],
            device_id={"sub": sub + 1 - 2 * side, "panel": panel},
            device_id_type=MESH,
        )

    @pl.when(sub < n_sub - 1)
    def _():
        halo_copy(0).start()

    @pl.when(sub > 0)
    def _():
        halo_copy(1).start()

    def transposed(b, carry):
        for q in range(per_panel * LOW):
            lhs[
                panel * per_panel + q // LOW,
                q % LOW,
                pl.ds(0, mode_rows),
                pl.ds(pl.multiple_of(b * tile, tile), tile),
            ] = jnp.transpose(ext[halo + b, :, pl.ds(q * mode_rows, mode_rows)])
        return carry

    lax.fori_loop(0, block_rows, transposed, 0)

    def panel_copy(step, owner):
        block = lhs.at[
            pl.ds(owner * per_panel, per_panel), :, pl.ds(0, mode_rows), :
        ]
        return pltpu.make_async_remote_copy(
            src_ref=block,
            dst_ref=block,
            send_sem=pan_send.at[step],
            recv_sem=pan_recv.at[step],
            device_id={"sub": sub, "panel": lax.rem(panel + step, n_panel)},
            device_id_type=MESH,
        )

    for step in range(1, n_panel):
        panel_copy(step, panel).start()

    listed = rows_ref.shape[1]
    onehot[...] = (
        lax.broadcasted_iota(jnp.int32, (rows, listed), 0) == rows_ref[...]
    ).astype(jnp.float32).astype(jnp.bfloat16)
    wanted = LOW * IF_DEV

    def select(h, carry):
        place = lax.broadcasted_iota(jnp.int32, (wanted, listed), 0) + h * wanted
        hit = (place == target_ref[...]).astype(jnp.float32).astype(jnp.bfloat16)
        found = lax.dot_general(
            hit,
            onehot[...],
            (((1,), (1,)), ((), ())),
            preferred_element_type=jnp.float32,
        ).astype(jnp.bfloat16)
        for q in range(LOW):
            lhs[h, q, pl.ds(mode_rows, IF_DEV), :] = found[
                q * IF_DEV : (q + 1) * IF_DEV
            ]
        return carry

    lax.fori_loop(0, high, select, 0)
    tile_copy.wait()

    @pl.when(sub > 0)
    def _():
        halo_copy(0).wait_recv()

    @pl.when(sub < n_sub - 1)
    def _():
        halo_copy(1).wait_recv()

    def block_row(b, carry):
        count = counts_ref[0, b]
        left = jnp.concatenate(
            [
                jnp.where(j < count, tiles[b, j].astype(jnp.float32), 0.0).astype(
                    jnp.bfloat16
                )
                for j in range(slots)
            ],
            axis=1,
        )
        right = jnp.concatenate([ext[cols_ref[b, j]] for j in range(slots)], axis=0)
        kphi[pl.ds(pl.multiple_of(b * tile, tile), tile), :] = jnp.dot(
            left, right, preferred_element_type=jnp.float32
        ).astype(jnp.bfloat16)
        return carry

    lax.fori_loop(0, block_rows, block_row, 0)

    for step in range(1, n_panel):
        panel_copy(step, lax.rem(panel + n_panel - step, n_panel)).wait_recv()

    def first_copy(k):
        return pltpu.make_async_remote_copy(
            src_ref=s1_out.at[k],
            dst_ref=s1_in.at[k],
            send_sem=s1_send.at[k],
            recv_sem=s1_recv.at[k],
            device_id={"sub": first_peer, "panel": panel},
            device_id_type=MESH,
        )

    def second_copy(k):
        return pltpu.make_async_remote_copy(
            src_ref=s2_out.at[k],
            dst_ref=s2_in.at[k],
            send_sem=s2_send.at[k],
            recv_sem=s2_recv.at[k],
            device_id={"sub": second_peer, "panel": panel},
            device_id_type=MESH,
        )

    def third_copy(k, slot):
        return pltpu.make_async_remote_copy(
            src_ref=z_out.at[k],
            dst_ref=z_in.at[slot],
            send_sem=z_send.at[k],
            recv_sem=z_recv.at[slot],
            device_id={"sub": lax.rem(my_high + 1 + k, high) * LOW + low, "panel": panel},
            device_id_type=MESH,
        )

    chunk = min(256, width)

    def step_of(t, carry):
        @pl.when(t < high)
        def _():
            h = lax.rem(my_high + 1 + t, high)

            def columns(c, inner):
                at = pl.ds(pl.multiple_of(c * chunk, chunk), chunk)
                product = jnp.dot(
                    lhs[h].reshape(LOW * out_rows, rows),
                    kphi[:, at],
                    preferred_element_type=jnp.float32,
                )
                part[t, :, :, at] = product.reshape(LOW, out_rows, chunk)
                return inner

            lax.fori_loop(0, width // chunk, columns, 0)
            for j in range(2):
                q = (1 - first_bit) * first_weight + j * second_weight
                s1_out[t, j] = part[t, q].astype(jnp.bfloat16)
            first_copy(t).start()

        @pl.when((t >= 1) & (t < high + 1))
        def _():
            k = t - 1
            first_copy(k).wait_recv()
            q = first_bit * first_weight + (1 - second_bit) * second_weight
            s2_out[k] = (
                part[k, q] + s1_in[k, 1 - second_bit].astype(jnp.float32)
            ).astype(jnp.bfloat16)
            second_copy(k).start()

        @pl.when(t >= 2)
        def _():
            k = t - 2
            second_copy(k).wait_recv()
            total = (
                part[k, low]
                + s1_in[k, second_bit].astype(jnp.float32)
                + s2_in[k].astype(jnp.float32)
            )

            @pl.when(k < high - 1)
            def _():
                z_out[k] = total.astype(jnp.bfloat16)
                third_copy(k, my_high).start()

            @pl.when(k == high - 1)
            def _():
                red_ref[...] = total[:mode_rows]
                load_ref[...] = total[mode_rows:]

        return carry

    lax.fori_loop(0, high + 2, step_of, 0)

    def gathered(k, carry):
        slot = lax.rem(my_high + 1 + k, high)
        third_copy(k, slot).wait_recv()
        value = z_in[slot].astype(jnp.float32)
        red_ref[...] += value[:mode_rows]
        load_ref[...] += value[mode_rows:]
        third_copy(k, my_high).wait_send()
        return carry

    lax.fori_loop(0, high - 1, gathered, 0)

    def drained(k, carry):
        first_copy(k).wait_send()
        second_copy(k).wait_send()
        return carry

    lax.fori_loop(0, high, drained, 0)
    for step in range(1, n_panel):
        panel_copy(step, panel).wait_send()

    @pl.when(sub < n_sub - 1)
    def _():
        halo_copy(0).wait_send()

    @pl.when(sub > 0)
    def _():
        halo_copy(1).wait_send()


def body(
    n_sub,
    n_panel,
    stiffness_tiles,
    tile_columns,
    tile_counts,
    phi_modes,
    halo_to_right,
    halo_to_left,
    liner_rows,
    liner_owner,
    liner_slot,
):
    block_rows, slots, tile, _ = stiffness_tiles.shape
    rows, width = phi_modes.shape
    high = n_sub // LOW
    mode_rows = width * n_panel // n_sub
    out_rows = mode_rows + IF_DEV
    halo = halo_to_right.shape[0]
    listed = liner_rows.shape[0]
    target = (liner_owner[:, 0] * IF_DEV + liner_slot).reshape(1, listed)
    bf16, f32 = jnp.bfloat16, jnp.float32
    smem = pl.BlockSpec(memory_space=pltpu.SMEM)
    vmem = pl.BlockSpec(memory_space=pltpu.VMEM)
    hbm = pl.BlockSpec(memory_space=pl.ANY)
    dma = pltpu.SemaphoreType.DMA
    return pl.pallas_call(
        functools.partial(kernel, n_sub, n_panel),
        out_shape=(
            jax.ShapeDtypeStruct((mode_rows, width), f32),
            jax.ShapeDtypeStruct((IF_DEV, width), f32),
        ),
        in_specs=[smem, smem, smem, smem, vmem, vmem, hbm, hbm],
        out_specs=(vmem, vmem),
        scratch_shapes=[
            pltpu.VMEM((block_rows + 2 * halo, tile, width), bf16),
            pltpu.VMEM((block_rows, slots, tile, tile), bf16),
            pltpu.VMEM((rows, listed), bf16),
            pltpu.VMEM((high, LOW, out_rows, rows), bf16),
            pltpu.VMEM((rows, width), bf16),
            pltpu.VMEM((high, LOW, out_rows, width), f32),
            pltpu.VMEM((2, halo, tile, width), bf16),
            pltpu.VMEM((high, 2, out_rows, width), bf16),
            pltpu.VMEM((high, 2, out_rows, width), bf16),
            pltpu.VMEM((high, out_rows, width), bf16),
            pltpu.VMEM((high, out_rows, width), bf16),
            pltpu.VMEM((high, out_rows, width), bf16),
            pltpu.VMEM((high, out_rows, width), bf16),
            dma((2,)),
            dma((2,)),
            dma((2,)),
            dma((n_panel,)),
            dma((n_panel,)),
            dma((high,)),
            dma((high,)),
            dma((high,)),
            dma((high,)),
            dma((high,)),
            dma((high,)),
        ],
        compiler_params=pltpu.CompilerParams(
            collective_id=0, has_side_effects=True, vmem_limit_bytes=60 << 20
        ),
    )(
        tile_columns,
        tile_counts,
        halo_to_right,
        halo_to_left,
        liner_rows.reshape(1, listed),
        target,
        stiffness_tiles,
        phi_modes.reshape(block_rows, tile, width),
    )


def solution(mesh):
    return jax.shard_map(
        functools.partial(body, mesh.shape["sub"], mesh.shape["panel"]),
        mesh=mesh,
        in_specs=(
            P("sub", None, None, None),
            P("sub", None),
            P("sub", None),
            P("sub", "panel"),
            P("sub"),
            P("sub"),
            P("sub"),
            P("sub", None),
            P("sub"),
        ),
        out_specs=(P("sub", "panel"), P("sub", "panel")),
        check_vma=False,
    )
```

time: 292 us -> 106 us (0.36)
  waiting for transfers between devices: 186 us -> 0 us
  Pallas kernels: 0 us -> 96.4 us
  matrix products: 33.2 us -> 0 us
  local copies, waits for them, and re-layouts: 30.7 us -> 4.81 us
  starting transfers between devices: 19.1 us -> 0 us
  between operations: 14.2 us -> 0.64 us
  other arithmetic: 8.1 us -> 1.95 us
    reduce_scatter x1 -> x0, waiting for transfers between devices: 136 us -> none  [body(): lax.psum_scatter(partial_value, 'sub', scatter_dimension=0, tiled=True)]
    pallas_call x0 -> x1, Pallas kernels: none -> 96.4 us  [body(): pl.pallas_call(functools.partial(kernel, n_sub, n_panel), out_shape=(jax....]
    dot_general x4 -> x0, matrix products: 33.2 us -> none  [the longest x1 15.9 us: body(): jnp.einsum('bjrc,bjcw->brw', stiffness_tiles, chosen, preferred_element_t...]
    all_to_all x2 -> x0, waiting for transfers between devices: 30.4 us -> none  [the longest x1 30.4 us: body(): lax.all_to_all(outbox, 'sub', split_axis=0, concat_axis=0, tiled=True)]
    gather x4 -> x0, local copies, waits for them, and re-layouts: 26.4 us -> none  [the longest x1 15.3 us: body(): extended[tile_columns]]
    ppermute x2 -> x0, waiting for transfers between devices: 18.7 us -> none  [shifted(): lax.ppermute(value, axis, [(source, source + steps) for source in range(i...]
    all_to_all x2 -> x0, starting transfers between devices: 13.2 us -> none  [the longest x1 6.98 us: body(): lax.all_to_all(outbox, 'sub', split_axis=0, concat_axis=0, tiled=True)]
    ppermute x2 -> x0, starting transfers between devices: 5.83 us -> none  [shifted(): lax.ppermute(value, axis, [(source, source + steps) for source in range(i...]
  transfers between devices with their start and end apart: 6 -> 0, of which waited for: 4 -> 0; matrix products, arithmetic and copies ran while one was open for 19% -> 0% of each run, Pallas kernels for 0% -> 0%
where the time goes in v1:
time: 106 us; the launch traced here: 104 us
  Pallas kernels  96.4 us (91%)
  local copies, waits for them, and re-layouts  4.81 us (5%)
  other arithmetic  1.95 us (2%)
    pallas_call x1, Pallas kernels, body(): pl.pallas_call(functools.partial(kernel, n_sub, n_panel), out_shape=(jax....  96.4 us
    unnamed x3, local copies, waits for them, and re-layouts  4.81 us

profile of v1, /device:TPU:10, one launch (start us, length us, event | category | flops | bytes accessed | tf_op | source)
XLA Modules:
  0.0 103.7 jit_solution(7494920199832288617)
XLA Ops:
  0.6 0.7 broadcast_multiply_fusion
  1.3 1.3 %add.3 = s32[512]{0:T(512)} add(s32[512]{0:T(512)S(1)} %bitcast.6, s32[512]{0:T(512)} %param.17) | non-fusion elementwise | flops 512 | bytes 6144 | tf_op jit(solution)/shard_map/add | solution.py:351
  2.6 1.4 %copy.11.cols_ref = s32[16,8]{1,0:T(8,128)} copy(s32[16,8]{0,1:T(8,128)} %param.10) | data formatting | bytes 1024 | tf_op args[1]
  3.9 96.4 %shard_map.104 = (f32[128,1024]{1,0:T(8,128)}, f32[32,1024]{1,0:T(8,128)}) custom-call(s32[16,8]{1,0:T(8,128)} %copy.11.cols_ref, s32[1,16]{1,0:T(1,128)} %counts_ref.1, s32[2]{0:T(128)} %to_right_ref.1, s32[2]{0:T(128)} %to_left_ref.1, s32[1,512]{1,0:T(1,128)} %bitcast.7, s32[1,512]{1,0:T(1,128)} %bitcast.5, bf16[16,8,128,128]{3,2,1,0:T(8,128)(2,1)} %tiles_hbm.1, ...), custom_call_target="tpu_custom_call" | custom-call | tf_op jit(solution)/shard_map/pallas_call | solution.py:357
  100.3 1.9 %copy.14 = f32[128,1024]{1,0:T(8,128)} copy(f32[128,1024]{1,0:T(8,128)} %get-tuple-element.4) | data formatting | bytes 1048576
  102.2 1.6 %copy.15 = f32[32,1024]{1,0:T(8,128)} copy(f32[32,1024]{1,0:T(8,128)} %get-tuple-element.5) | data formatting | bytes 262144

commit v2 on v1

v2 whole, which is shorter than its diff:
```python
import functools

import jax
import jax.numpy as jnp
from jax import lax
from jax.experimental import pallas as pl
from jax.experimental.pallas import tpu as pltpu
from jax.sharding import PartitionSpec as P

IF_DEV = 32
LOW = 4
PARTS = 2
MESH = pl.DeviceIdType.MESH


def kernel(
    n_sub,
    n_panel,
    cols_ref,
    counts_ref,
    to_right_ref,
    to_left_ref,
    rows_ref,
    target_ref,
    tiles_hbm,
    phi_hbm,
    red_ref,
    load_ref,
    ext,
    tiles,
    onehot,
    lhs,
    kphi,
    part,
    halo_out,
    halo_in,
    s1_out,
    s1_in,
    s2_out,
    s2_in,
    z_out,
    z_in,
    local_sem,
    halo_send,
    halo_recv,
    pan_send,
    pan_recv,
    s1_send,
    s1_recv,
    s2_send,
    s2_recv,
    z_send,
    z_recv,
):
    block_rows, slots, tile, _ = tiles.shape
    halo = halo_out.shape[2]
    rows = block_rows * tile
    width = kphi.shape[2]
    high = n_sub // LOW
    mode_rows = red_ref.shape[0]
    out_rows = mode_rows + IF_DEV
    per_panel = high // n_panel
    sub = lax.axis_index("sub")
    panel = lax.axis_index("panel")
    low, my_high = lax.rem(sub, LOW), sub // LOW
    bit0, bit1 = lax.rem(low, 2), low // 2

    def order(part_of):
        swap = 1 - part_of * (1 - lax.rem(panel, 2))
        first_bit = (1 - swap) * bit0 + swap * bit1
        second_bit = (1 - swap) * bit1 + swap * bit0
        first_weight, second_weight = 1 + swap, 2 - swap
        first_peer = sub + (1 - 2 * first_bit) * first_weight
        second_peer = sub + (1 - 2 * second_bit) * second_weight
        return first_bit, second_bit, first_weight, second_weight, first_peer, second_peer

    barrier = pltpu.get_barrier_semaphore()

    def greet(place):
        pl.semaphore_signal(barrier, inc=1, device_id=place, device_id_type=MESH)

    greet({"sub": sub + 1 - 2 * bit0, "panel": panel})
    greet({"sub": sub + 2 - 4 * bit1, "panel": panel})

    @pl.when(sub > 0)
    def _():
        greet({"sub": sub - 1, "panel": panel})

    @pl.when(sub < n_sub - 1)
    def _():
        greet({"sub": sub + 1, "panel": panel})

    for step in range(1, n_panel):
        greet({"sub": sub, "panel": lax.rem(panel + step, n_panel)})
    for step in range(1, high):
        greet({"sub": lax.rem(my_high + step, high) * LOW + low, "panel": panel})

    phi_copies = [
        pltpu.make_async_copy(
            phi_hbm.at[:, :, pl.ds(c * width, width)],
            ext.at[c, pl.ds(halo, block_rows)],
            local_sem.at[c],
        )
        for c in range(PARTS)
    ]
    tile_copy = pltpu.make_async_copy(tiles_hbm, tiles, local_sem.at[PARTS])
    for copy in phi_copies:
        copy.start()
    tile_copy.start()
    for copy in phi_copies:
        copy.wait()
    for c in range(PARTS):
        for i in range(halo):
            halo_out[c, 0, i] = ext[c, halo + to_right_ref[i]]
            halo_out[c, 1, i] = ext[c, halo + to_left_ref[i]]
    ends = jnp.where(sub > 0, 1, 0) + jnp.where(sub < n_sub - 1, 1, 0)
    pl.semaphore_wait(barrier, 2 + (n_panel - 1) + (high - 1) + ends)

    def halo_copy(c, side):
        return pltpu.make_async_remote_copy(
            src_ref=halo_out.at[c, side],
            dst_ref=halo_in.at[c, side],
            send_sem=halo_send.at[c, side],
            recv_sem=halo_recv.at[c, side],
            device_id={"sub": sub + 1 - 2 * side, "panel": panel},
            device_id_type=MESH,
        )

    def send_halo(c):
        @pl.when(sub < n_sub - 1)
        def _():
            halo_copy(c, 0).start()

        @pl.when(sub > 0)
        def _():
            halo_copy(c, 1).start()

    send_halo(0)

    def transposed(b, carry):
        for q in range(per_panel * LOW):
            lhs[
                panel * per_panel + q // LOW,
                q % LOW,
                pl.ds(0, mode_rows),
                pl.ds(pl.multiple_of(b * tile, tile), tile),
            ] = jnp.transpose(
                ext[
                    q * mode_rows // width,
                    halo + b,
                    :,
                    pl.ds(q * mode_rows % width, mode_rows),
                ]
            )
        return carry

    lax.fori_loop(0, block_rows, transposed, 0)

    def panel_copy(step, owner):
        block = lhs.at[
            pl.ds(owner * per_panel, per_panel), :, pl.ds(0, mode_rows), :
        ]
        return pltpu.make_async_remote_copy(
            src_ref=block,
            dst_ref=block,
            send_sem=pan_send.at[step],
            recv_sem=pan_recv.at[step],
            device_id={"sub": sub, "panel": lax.rem(panel + step, n_panel)},
            device_id_type=MESH,
        )

    for step in range(1, n_panel):
        panel_copy(step, panel).start()

    listed = rows_ref.shape[1]
    onehot[...] = (
        lax.broadcasted_iota(jnp.int32, (rows, listed), 0) == rows_ref[...]
    ).astype(jnp.float32).astype(jnp.bfloat16)
    wanted = LOW * IF_DEV

    def select(h, carry):
        place = lax.broadcasted_iota(jnp.int32, (wanted, listed), 0) + h * wanted
        hit = (place == target_ref[...]).astype(jnp.float32).astype(jnp.bfloat16)
        found = lax.dot_general(
            hit,
            onehot[...],
            (((1,), (1,)), ((), ())),
            preferred_element_type=jnp.float32,
        ).astype(jnp.bfloat16)
        for q in range(LOW):
            lhs[h, q, pl.ds(mode_rows, IF_DEV), :] = found[
                q * IF_DEV : (q + 1) * IF_DEV
            ]
        return carry

    lax.fori_loop(0, high, select, 0)
    tile_copy.wait()

    def products(c):
        for side in range(2):
            there = sub > 0 if side == 0 else sub < n_sub - 1
            place = pl.ds(side * (halo + block_rows), halo)

            @pl.when(there)
            def _(side=side, place=place):
                halo_copy(c, side).wait_recv()
                ext[c, place] = halo_in[c, side]

            @pl.when(jnp.logical_not(there))
            def _(place=place):
                ext[c, place] = jnp.zeros((halo, tile, width), ext.dtype)

        if c + 1 < PARTS:
            send_halo(c + 1)

        def block_row(b, carry):
            count = counts_ref[0, b]
            left = jnp.concatenate(
                [
                    jnp.where(j < count, tiles[b, j].astype(jnp.float32), 0.0).astype(
                        jnp.bfloat16
                    )
                    for j in range(slots)
                ],
                axis=1,
            )
            right = jnp.concatenate(
                [ext[c, cols_ref[j, b]] for j in range(slots)], axis=0
            )
            kphi[c, pl.ds(pl.multiple_of(b * tile, tile), tile), :] = jnp.dot(
                left, right, preferred_element_type=jnp.float32
            ).astype(jnp.bfloat16)
            return carry

        lax.fori_loop(0, block_rows, block_row, 0)

    products(0)

    for step in range(1, n_panel):
        panel_copy(step, lax.rem(panel + n_panel - step, n_panel)).wait_recv()

    def first_copy(k):
        return pltpu.make_async_remote_copy(
            src_ref=s1_out.at[k],
            dst_ref=s1_in.at[k],
            send_sem=s1_send.at[k],
            recv_sem=s1_recv.at[k],
            device_id={"sub": order(k // high)[4], "panel": panel},
            device_id_type=MESH,
        )

    def second_copy(k):
        return pltpu.make_async_remote_copy(
            src_ref=s2_out.at[k],
            dst_ref=s2_in.at[k],
            send_sem=s2_send.at[k],
            recv_sem=s2_recv.at[k],
            device_id={"sub": order(k // high)[5], "panel": panel},
            device_id_type=MESH,
        )

    def third_copy(k, slot):
        return pltpu.make_async_remote_copy(
            src_ref=z_out.at[k],
            dst_ref=z_in.at[slot],
            send_sem=z_send.at[k],
            recv_sem=z_recv.at[slot],
            device_id={
                "sub": lax.rem(my_high + 1 + lax.rem(k, high), high) * LOW + low,
                "panel": panel,
            },
            device_id_type=MESH,
        )

    chunk = min(256, width)

    total_steps = PARTS * high
    lag = 3

    def step_of(t, carry):
        for c in range(1, PARTS):

            @pl.when(t == c * high)
            def _(c=c):
                products(c)

        @pl.when(t < total_steps)
        def _():
            c = t // high
            h = lax.rem(my_high + 1 + lax.rem(t, high), high)
            first_bit, _, first_weight, second_weight, _, _ = order(c)

            def columns(i, inner):
                at = pl.ds(pl.multiple_of(i * chunk, chunk), chunk)
                product = jnp.dot(
                    lhs[h].reshape(LOW * out_rows, rows),
                    kphi[c, :, at],
                    preferred_element_type=jnp.float32,
                )
                part[t, :, :, at] = product.reshape(LOW, out_rows, chunk)
                return inner

            lax.fori_loop(0, width // chunk, columns, 0)
            for j in range(2):
                q = (1 - first_bit) * first_weight + j * second_weight
                s1_out[t, j] = part[t, q].astype(jnp.bfloat16)
            first_copy(t).start()

        @pl.when((t >= lag) & (t < total_steps + lag))
        def _():
            k = t - lag
            first_bit, second_bit, first_weight, second_weight, _, _ = order(k // high)
            first_copy(k).wait_recv()
            q = first_bit * first_weight + (1 - second_bit) * second_weight
            s2_out[k] = (
                part[k, q] + s1_in[k, 1 - second_bit].astype(jnp.float32)
            ).astype(jnp.bfloat16)
            second_copy(k).start()

        @pl.when(t >= lag + 1)
        def _():
            k = t - lag - 1
            _, second_bit, _, _, _, _ = order(k // high)
            second_copy(k).wait_recv()
            total = (
                part[k, low]
                + s1_in[k, second_bit].astype(jnp.float32)
                + s2_in[k].astype(jnp.float32)
            )

            @pl.when(lax.rem(k, high) < high - 1)
            def _():
                z_out[k] = total.astype(jnp.bfloat16)
                third_copy(k, k // high * high + my_high).start()

            for c in range(PARTS):

                @pl.when(k == (c + 1) * high - 1)
                def _(c=c):
                    red_ref[:, pl.ds(c * width, width)] = total[:mode_rows]
                    load_ref[:, pl.ds(c * width, width)] = total[mode_rows:]

        return carry

    lax.fori_loop(0, total_steps + lag + 1, step_of, 0)

    for c in range(PARTS):
        at_part = pl.ds(c * width, width)

        def gathered(k, carry, c=c, at_part=at_part):
            slot = c * high + lax.rem(my_high + 1 + k, high)
            third_copy(c * high + k, slot).wait_recv()
            value = z_in[slot].astype(jnp.float32)
            red_ref[:, at_part] += value[:mode_rows]
            load_ref[:, at_part] += value[mode_rows:]
            third_copy(c * high + k, slot).wait_send()
            return carry

        lax.fori_loop(0, high - 1, gathered, 0)

    def drained(k, carry):
        first_copy(k).wait_send()
        second_copy(k).wait_send()
        return carry

    lax.fori_loop(0, total_steps, drained, 0)
    for step in range(1, n_panel):
        panel_copy(step, panel).wait_send()

    for c in range(PARTS):

        @pl.when(sub < n_sub - 1)
        def _(c=c):
            halo_copy(c, 0).wait_send()

        @pl.when(sub > 0)
        def _(c=c):
            halo_copy(c, 1).wait_send()


def body(
    n_sub,
    n_panel,
    stiffness_tiles,
    tile_columns,
    tile_counts,
    phi_modes,
    halo_to_right,
    halo_to_left,
    liner_rows,
    liner_owner,
    liner_slot,
):
    block_rows, slots, tile, _ = stiffness_tiles.shape
    rows, width = phi_modes.shape
    high = n_sub // LOW
    mode_rows = width * n_panel // n_sub
    out_rows = mode_rows + IF_DEV
    halo = halo_to_right.shape[0]
    half = width // PARTS
    listed = liner_rows.shape[0]
    target = (liner_owner[:, 0] * IF_DEV + liner_slot).reshape(1, listed)
    bf16, f32 = jnp.bfloat16, jnp.float32
    smem = pl.BlockSpec(memory_space=pltpu.SMEM)
    vmem = pl.BlockSpec(memory_space=pltpu.VMEM)
    hbm = pl.BlockSpec(memory_space=pl.ANY)
    dma = pltpu.SemaphoreType.DMA
    return pl.pallas_call(
        functools.partial(kernel, n_sub, n_panel),
        out_shape=(
            jax.ShapeDtypeStruct((mode_rows, width), f32),
            jax.ShapeDtypeStruct((IF_DEV, width), f32),
        ),
        in_specs=[smem, smem, smem, smem, vmem, vmem, hbm, hbm],
        out_specs=(vmem, vmem),
        scratch_shapes=[
            pltpu.VMEM((PARTS, block_rows + 2 * halo, tile, half), bf16),
            pltpu.VMEM((block_rows, slots, tile, tile), bf16),
            pltpu.VMEM((rows, listed), bf16),
            pltpu.VMEM((high, LOW, out_rows, rows), bf16),
            pltpu.VMEM((PARTS, rows, half), bf16),
            pltpu.VMEM((PARTS * high, LOW, out_rows, half), f32),
            pltpu.VMEM((PARTS, 2, halo, tile, half), bf16),
            pltpu.VMEM((PARTS, 2, halo, tile, half), bf16),
            pltpu.VMEM((PARTS * high, 2, out_rows, half), bf16),
            pltpu.VMEM((PARTS * high, 2, out_rows, half), bf16),
            pltpu.VMEM((PARTS * high, out_rows, half), bf16),
            pltpu.VMEM((PARTS * high, out_rows, half), bf16),
            pltpu.VMEM((PARTS * high, out_rows, half), bf16),
            pltpu.VMEM((PARTS * high, out_rows, half), bf16),
            dma((PARTS + 1,)),
            dma((PARTS, 2)),
            dma((PARTS, 2)),
            dma((n_panel,)),
            dma((n_panel,)),
        ]
        + [dma((PARTS * high,))] * 6,
        compiler_params=pltpu.CompilerParams(
            collective_id=0, has_side_effects=True, vmem_limit_bytes=60 << 20
        ),
    )(
        tile_columns.T,
        tile_counts,
        halo_to_right,
        halo_to_left,
        liner_rows.reshape(1, listed),
        target,
        stiffness_tiles,
        phi_modes.reshape(block_rows, tile, width),
    )


def solution(mesh):
    return jax.shard_map(
        functools.partial(body, mesh.shape["sub"], mesh.shape["panel"]),
        mesh=mesh,
        in_specs=(
            P("sub", None, None, None),
            P("sub", None),
            P("sub", None),
            P("sub", "panel"),
            P("sub"),
            P("sub"),
            P("sub"),
            P("sub", None),
            P("sub"),
        ),
        out_specs=(P("sub", "panel"), P("sub", "panel")),
        check_vma=False,
    )
```

time: 106 us -> 94.5 us (0.89); the launches traced: 104 us -> 94.2 us
  Pallas kernels: 96.4 us -> 88.2 us
  local copies, waits for them, and re-layouts: 4.81 us -> 3.45 us
    pallas_call x1, Pallas kernels: 96.4 us -> 88.2 us  [body(): pl.pallas_call(functools.partial(kernel, n_sub, n_panel), out_shape=(jax....]
    unnamed x3 -> x2, local copies, waits for them, and re-layouts: 4.81 us -> 3.45 us
where the time goes in v2:
time: 94.5 us; the launch traced here: 94.2 us
  Pallas kernels  88.2 us (93%)
  local copies, waits for them, and re-layouts  3.45 us (4%)
  other arithmetic  1.95 us (2%)
    pallas_call x1, Pallas kernels, body(): pl.pallas_call(functools.partial(kernel, n_sub, n_panel), out_shape=(jax....  88.2 us
    unnamed x2, local copies, waits for them, and re-layouts  3.45 us

profile of v2, /device:TPU:10, one launch (start us, length us, event | category | flops | bytes accessed | tf_op | source)
XLA Modules:
  0.0 94.2 jit_solution(11301987054273080225)
XLA Ops:
  0.6 0.7 broadcast_multiply_fusion
  1.3 1.3 %add.3 = s32[512]{0:T(512)} add(s32[512]{0:T(512)S(1)} %bitcast.6, s32[512]{0:T(512)} %param.17) | non-fusion elementwise | flops 512 | bytes 6144 | tf_op jit(solution)/shard_map/add | solution.py:402
  2.6 88.2 %shard_map.104 = (f32[128,1024]{1,0:T(8,128)}, f32[32,1024]{1,0:T(8,128)}) custom-call(s32[8,16]{1,0:T(8,128)} %bitcast.8, s32[1,16]{1,0:T(1,128)} %counts_ref.1, s32[2]{0:T(128)} %to_right_ref.1, s32[2]{0:T(128)} %to_left_ref.1, s32[1,512]{1,0:T(1,128)} %bitcast.9, s32[1,512]{1,0:T(1,128)} %bitcast.7, bf16[16,8,128,128]{3,2,1,0:T(8,128)(2,1)} %tiles_hbm.1, ...), custom_call_target="tpu_custom_call" | custom-call | tf_op jit(solution)/shard_map/pallas_call | solution.py:408
  90.7 1.9 %copy.13 = f32[128,1024]{1,0:T(8,128)} copy(f32[128,1024]{1,0:T(8,128)} %get-tuple-element.4) | data formatting | bytes 1048576
  92.6 1.6 %copy.14 = f32[32,1024]{1,0:T(8,128)} copy(f32[32,1024]{1,0:T(8,128)} %get-tuple-element.5) | data formatting | bytes 262144
